TPU v7x, 32 devices: a whole 2x2x4 slice. The times are simulated.
32 devices in a mesh: leaf: 8 (over z, core), gen: 4 (over y, x).
Axes of the slice: x: 2, y: 2, z: 4, core: 2. Of those that a mesh axis runs over, the one named last changes fastest.
Arguments:
- points: float32 [16, 8, 2, 512], P(None, 'leaf'), may hold values from 0 to 1
- generators: bfloat16 [16, 8, 2, 512, 128], P(None, 'leaf', None, 'gen'), may hold values from -6 to 6
- leaf_ranks: int32 [16, 8], P(None, 'leaf'), may hold values from 112 to 128
- translations: bfloat16 [16, 8, 128, 256], P(None, 'leaf'), may hold values from -0.5 to 0.5
- parent_ranks: int32 [8, 8], P(None, 'leaf'), may hold values from 128 to 160
Outputs:
- leaf_basis: float32 [16, 8, 2, 512, 128], P(None, 'leaf', None, 'gen')
- leaf_block: float32 [16, 8, 128, 128], P(None, 'leaf', 'gen')
- parent_basis: float32 [8, 8, 256, 256], P(None, 'leaf', 'gen')
- parent_block: float32 [8, 8, 256, 256], P(None, 'leaf', 'gen')
Inputs may be any that keep to these rules, and one draw needn't show every extreme that they name: `leaf_ranks`: a leaf's rank; generator columns from the rank on are ignored. `parent_ranks`: a parent's rank; translation columns from the rank on are ignored.
All inputs are finite; a program needn't handle non-finite values.
Results may differ from a plain program's by a relative error of at most 0.0003.
Values may be sent and summed in bfloat16 or wider, within the bound.
A program may use at most 128 MiB of HBM per device.

v0:
```python
import jax
import jax.numpy as jnp
from jax import lax
from jax.sharding import PartitionSpec as P

HIGHEST = lax.Precision.HIGHEST
RANGE_SCALE = 4.0
SIGMA_ONE = 1.0
SIGMA_TWO = 0.8
CROSS_CORR = 0.5
NUGGET = 0.1


def swapped(array, axis, apart):
    return lax.ppermute(array, axis, [(i, i ^ 1 << apart) for i in range(lax.axis_size(axis))])


def matern(first, second):
    across = first[..., 0, :, None] - second[..., 0, None, :]
    upward = first[..., 1, :, None] - second[..., 1, None, :]
    scaled = RANGE_SCALE * jnp.sqrt(across * across + upward * upward)
    decays = jnp.exp(-scaled)
    marginal_one = SIGMA_ONE * SIGMA_ONE * decays
    middle = CROSS_CORR * SIGMA_ONE * SIGMA_TWO * (1.0 + scaled) * decays
    smooth = SIGMA_TWO * SIGMA_TWO * (1.0 + scaled + scaled * scaled / 3.0) * decays
    top_row = jnp.stack([marginal_one, middle], -2)
    bottom_row = jnp.stack([middle, smooth], -2)
    return jnp.stack([top_row, bottom_row], -4)


def kernel_apply(near_coords, far_coords, far_columns):
    return jnp.einsum(
        "vnwp,wpk->vnk", matern(near_coords, far_coords), far_columns, precision=HIGHEST
    )


def one_product(member):
    near_coords, far_coords, far_columns = member
    return kernel_apply(near_coords, far_coords, far_columns.astype(jnp.float32))


def lower_inverse(matrix):
    factor_low = jnp.linalg.cholesky(matrix)
    identity = jnp.broadcast_to(jnp.eye(matrix.shape[-1], dtype=jnp.float32), matrix.shape)
    return (factor_low, jax.scipy.linalg.solve_triangular(factor_low, identity, lower=True))


def per_device(points, generators, leaf_ranks, translations, parent_ranks):
    leaf_count = generators.shape[0]
    half_count = leaf_count // 2
    row_share = generators.shape[3]
    rank_width = generators.shape[-1]
    parent_width = translations.shape[-1]
    gen_count = lax.axis_size("gen")
    gen_spot = lax.axis_index("gen")
    parity = lax.axis_index("leaf") % 2
    keep_start = parity * half_count
    give_start = (1 - parity) * half_count

    def select_half(values, offset):
        return lax.dynamic_slice_in_dim(values, offset, half_count, 0)

    coords = points[:, 0]
    column_keep = (lax.iota(jnp.int32, rank_width)[None, :] < leaf_ranks[:, 0][:, None]).astype(
        jnp.float32
    )
    masked = generators[:, 0] * column_keep[:, None, None, :].astype(jnp.bfloat16)
    mapped = translations[:, 0] * column_keep[:, :, None].astype(jnp.bfloat16)
    far_coords = swapped(coords, "leaf", 0)
    own_far_coords = select_half(far_coords, keep_start)
    local_gram = jnp.einsum("lvnk,lvnj->lkj", masked, masked, preferred_element_type=jnp.float32)
    gram_sum = lax.psum(local_gram, "gen") + jax.vmap(jnp.diag)(1.0 - column_keep)
    lows, inverses = lower_inverse(gram_sum)
    bases = jnp.einsum(
        "lvnk,ljk->lvnj", masked, inverses, precision=HIGHEST, preferred_element_type=jnp.float32
    )
    far_shards, far_maps = swapped(
        (select_half(masked, give_start), select_half(mapped, give_start)), "leaf", 0
    )
    local_rows = lax.dynamic_slice_in_dim(coords, gen_spot * row_share, row_share, 2)
    own_rows = select_half(local_rows, keep_start)
    piece_own = lax.all_gather(masked, "gen", axis=2, tiled=True)
    piece_far = lax.all_gather(far_shards, "gen", axis=2, tiled=True)
    nearby = lax.map(one_product, (local_rows, coords, piece_own))
    across = lax.map(one_product, (own_rows, own_far_coords, piece_far))
    projected = jnp.einsum("lvnk,lvnj->lkj", bases, nearby, precision=HIGHEST)
    local_blocks = jnp.einsum("lkj,lij->lki", projected, inverses, precision=HIGHEST)
    local_blocks = local_blocks + NUGGET * jnp.einsum(
        "lvnk,lvnj->lkj", bases, bases, precision=HIGHEST
    )
    local_raw = jnp.einsum(
        "lvnk,lvnj->lkj", select_half(bases, keep_start), across, precision=HIGHEST
    )
    blocks, raw = lax.psum((local_blocks, local_raw), "gen")
    far_block, far_low = swapped(
        (select_half(blocks, give_start), select_half(lows, give_start)), "leaf", 0
    )
    far_identity = jnp.broadcast_to(jnp.eye(rank_width, dtype=jnp.float32), far_low.shape)
    far_inverse = jax.scipy.linalg.solve_triangular(far_low, far_identity, lower=True)
    coupled = jnp.einsum("lkj,lij->lki", raw, far_inverse, precision=HIGHEST)
    own_block = select_half(blocks, keep_start)
    own_low = select_half(lows, keep_start)
    own_factor = jnp.einsum(
        "lkj,lkp->ljp",
        own_low,
        select_half(mapped, keep_start).astype(jnp.float32),
        precision=HIGHEST,
    )
    far_factor = jnp.einsum(
        "lkj,lkp->ljp", far_low, far_maps.astype(jnp.float32), precision=HIGHEST
    )
    is_even = parity == 0
    even_block = jnp.where(is_even, own_block, far_block)
    odd_block = jnp.where(is_even, far_block, own_block)
    even_factor = jnp.where(is_even, own_factor, far_factor)
    odd_factor = jnp.where(is_even, far_factor, own_factor)
    coupled = jnp.where(is_even, coupled, jnp.swapaxes(coupled, 1, 2))
    parent_keep = (lax.iota(jnp.int32, parent_width)[None, :] < parent_ranks[:, 0][:, None]).astype(
        jnp.float32
    )
    stacked = jnp.concatenate([even_factor, odd_factor], 1) * parent_keep[:, None, :]
    parent_gram = jnp.einsum("lak,laj->lkj", stacked, stacked, precision=HIGHEST) + jax.vmap(
        jnp.diag
    )(1.0 - parent_keep)
    parent_low, parent_inverse = lower_inverse(parent_gram)
    parent_bases = jnp.einsum("lak,ljk->laj", stacked, parent_inverse, precision=HIGHEST)
    top_row = jnp.concatenate([even_block, coupled], 2)
    bottom_row = jnp.concatenate([jnp.swapaxes(coupled, 1, 2), odd_block], 2)
    parent_matrix = jnp.concatenate([top_row, bottom_row], 1)
    mixed = jnp.einsum("lab,lbj->laj", parent_matrix, parent_bases, precision=HIGHEST)
    parent_blocks = jnp.einsum("lak,laj->lkj", parent_bases, mixed, precision=HIGHEST)
    leaf_share = rank_width // gen_count
    basis_share = 2 * rank_width // gen_count
    parent_share = parent_width // gen_count
    leaf_out = lax.dynamic_slice_in_dim(blocks, gen_spot * leaf_share, leaf_share, 1)
    basis_out = lax.dynamic_slice_in_dim(parent_bases, gen_spot * basis_share, basis_share, 1)
    block_out = lax.dynamic_slice_in_dim(parent_blocks, gen_spot * parent_share, parent_share, 1)
    return (bases[:, None], leaf_out[:, None], basis_out[:, None], block_out[:, None])


def solution(mesh):
    return jax.shard_map(
        per_device,
        mesh=mesh,
        in_specs=(
            P(None, "leaf", None, None),
            P(None, "leaf", None, "gen", None),
            P(None, "leaf"),
            P(None, "leaf", None, None),
            P(None, "leaf"),
        ),
        out_specs=(
            P(None, "leaf", None, "gen", None),
            P(None, "leaf", "gen", None),
            P(None, "leaf", "gen", None),
            P(None, "leaf", "gen", None),
        ),
        check_vma=False,
    )
```

profile of v0, /device:TPU:0, one launch (start us, length us, event | category | flops | bytes accessed | tf_op | source)
XLA Modules:
  0.0 1115.4 jit_solution(18055530516305526337)
XLA Ops:
  22.6 44.4 %all-reduce.5.cloned.1.call-done = f32[16,128,128]{2,1,0:T(8,128)} async-done(((f32[16,128,128]{2,1,0:T(8,128)}), f32[16,128,128]{2,1,0:T(8,128)}) %all-reduce.5.cloned.1.call-update) | async-done | bytes 1048592 | tf_op jit(solution)/shard_map/psum | solution.py:72
  70.0 187.5 %custom-call.29 = f32[16,128,128]{2,1,0:T(8,128)S(1)} custom-call(f32[16,128,128]{2,1,0:T(8,128)S(1)} %fusion.38), custom_call_target="Cholesky" | custom-call | tf_op jit(solution)/shard_map/jit(cholesky)/cholesky | solution.py:43
  259.6 158.3 %custom-call.30 = f32[16,1,128,128]{2,3,1,0:T(8,128)S(1)} custom-call(f32[16,1,128,128]{3,2,1,0:T(8,128)} %get-tuple-element.108), custom_call_target="InvertDiagBlocksLowerTriangular" | custom-call | tf_op jit(solution)/shard_map/jit(_solve_triangular)/vmap()/triangular_solve | solution.py:45
  422.5 4.5 fusion.33
  430.0 4.9 fusion.32
  434.9 3.3 copy.33
  438.2 2.7 fusion.31
  443.1 95.2 %custom-call.31 = f32[8,128,128]{2,1,0:T(8,128)} custom-call(f32[8,128,128]{2,1,0:T(8,128)} %cholesky.142), custom_call_target="Cholesky" | custom-call | tf_op jit(solution)/shard_map/jit(cholesky)/cholesky | solution.py:43
  538.3 2.7 cholesky.138
  542.1 80.0 %custom-call.32 = f32[8,1,128,128]{2,3,1,0:T(8,128)} custom-call(f32[8,1,128,128]{3,2,1,0:T(8,128)} %get-tuple-element.140), custom_call_target="InvertDiagBlocksLowerTriangular" | custom-call | tf_op jit(solution)/shard_map/jit(cholesky)/cholesky | solution.py:43
  622.1 2.7 constant_dynamic-update-slice_fusion.1
  624.8 3.1 convolution_subtract_fusion.1
  627.9 95.4 %custom-call.33 = f32[8,128,128]{2,1,0:T(8,128)} custom-call(f32[8,128,128]{2,1,0:T(8,128)} %convolution_subtract_fusion.1), custom_call_target="Cholesky" | custom-call | tf_op jit(solution)/shard_map/jit(cholesky)/cholesky | solution.py:43
  725.7 3.2 select_select_fusion
  728.9 32.4 %while.22 = (s32[]{:T(128)}, f32[8,2,128,128]{3,2,1,0:T(8,128)}, f32[8,2,128]{2,1,0:T(2,128)}, f32[8,2,512]{2,1,0:T(2,128)}, bf16[8,2,512,128]{3,2,1,0:T(8,128)(2,1)}, /*index=5*/s32[]{:T(128)}, s32[]{:T(128)}, s32[]{}) while((s32[]{:T(128)}, f32[8,2,128,128]{3,2,1,0:T(8,128)}, f32[8,2,128]{2,1,0:T(2,128)}, f32[8,2,512]{2,1,0:T(2,128)}, ...), condition=%wide.region_11.12_spmd, body=%wide.region_10.11_spmd.sunk | while | flops 404160512 | bytes 4081781 | solution.py:85
  730.7 2.2 fusion.101
  734.8 2.2 fusion.101
  738.8 2.2 fusion.101
  742.9 2.2 fusion.101
  746.9 2.2 fusion.101
  750.9 2.2 fusion.101
  759.1 2.2 fusion.101
  761.3 3.9 convolution_bitcast_fusion.5
  765.2 65.0 %while.21 = (s32[]{:T(128)}, f32[16,2,128,128]{3,2,1,0:T(8,128)}, f32[16,2,128]{2,1,0:T(2,128)}, f32[16,2,512]{2,1,0:T(2,128)}, bf16[16,2,512,128]{3,2,1,0:T(8,128)(2,1)}, /*index=5*/s32[]{:T(128)}, s32[]{:T(128)}, s32[]{}) while((s32[]{:T(128)}, f32[16,2,128,128]{3,2,1,0:T(8,128)}, f32[16,2,128]{2,1,0:T(2,128)}, f32[16,2,512]{2,1,0:T(2,128)}, ...), condition=%wide.region_4.5_spmd, body=%wide.region_3.4_spmd.sunk | while | flops 404160512 | bytes 4081781 | solution.py:84
  767.0 2.2 fusion.98
  771.0 2.2 fusion.98
  779.2 2.2 fusion.98
  783.2 2.2 fusion.98
  787.3 2.2 fusion.98
  791.3 2.2 fusion.98
  795.4 2.2 fusion.98
  799.4 2.2 fusion.98
  803.5 2.2 fusion.98
  807.6 2.2 fusion.98
  811.6 2.2 fusion.98
  815.6 2.2 fusion.98
  819.7 2.2 fusion.98
  823.8 2.2 fusion.98
  827.8 2.2 fusion.98
  830.2 5.3 convolution_bitcast_fusion.3
  835.6 3.3 convolution_add_fusion
  839.1 5.8 while.23
  839.7 2.3 bitcast_dynamic-update-slice_fusion.2
  842.5 2.3 bitcast_dynamic-update-slice_fusion.2
  844.8 158.6 %custom-call.34 = f32[8,2,128,128]{2,3,1,0:T(8,128)} custom-call(f32[8,2,128,128]{3,2,1,0:T(8,128)} %bitcast.188), custom_call_target="InvertDiagBlocksLowerTriangular" | custom-call | tf_op jit(solution)/shard_map/jit(_solve_triangular)/vmap()/triangular_solve | solution.py:45
  1003.5 80.3 %custom-call.35 = f32[8,1,128,128]{2,3,1,0:T(8,128)} custom-call(f32[8,1,128,128]{3,2,1,0:T(8,128)} %get-tuple-element.139), custom_call_target="InvertDiagBlocksLowerTriangular" | custom-call | tf_op jit(solution)/shard_map/jit(_solve_triangular)/vmap()/triangular_solve | solution.py:99
  1094.5 2.3 fusion.66
  1104.1 3.5 fusion.67
  (263 shorter events, 101.4 us)
Async XLA Ops:
  7.2 59.8 %all-reduce.5.cloned.1.call-start = ((), (), s32[]{:S(2)}) async-start(), calls=%async_computation | async-start | bytes 2097152 | tf_op jit(solution)/shard_map/psum | solution.py:72
  9.2 1.6 copy-start.1
  10.7 3.8 copy-start.27
  10.7 4.3 copy-start.20
  10.7 718.1 %all-gather.5.cloned.1.call-start = ((), (), s32[]{:S(2)}) async-start(), calls=%async_computation.2 | async-start | bytes 2621440 | tf_op jit(solution)/shard_map/all_gather | solution.py:83
  10.9 2.1 collective-permute-start.4
  12.9 0.8 copy-start.21
  13.7 4.2 copy-start.28
  13.7 4.3 copy-start.29
  13.8 751.4 %all-gather.3.cloned.1.call-start = ((), (), s32[]{:S(2)}) async-start(), calls=%async_computation.1 | async-start | bytes 5242880 | tf_op jit(solution)/shard_map/all_gather | solution.py:82
  14.5 1077.7 %all-reduce.7.cloned.1.call-start = ((), (), s32[]{:S(2)}) async-start(), calls=%async_computation.3 | async-start | bytes 3145728 | tf_op jit(solution)/shard_map/psum | solution.py:94
  14.6 7.4 collective-permute-start.3
  15.3 1.0 copy-start.12
  17.2 409.9 %collective-permute-start.1 = (bf16[8,128,256]{2,1,0:T(8,128)(2,1)}, bf16[8,128,256]{2,1,0:T(8,128)(2,1)}, u32[]{:S(2)}, u32[]{:S(2)}) collective-permute-start(bf16[8,128,256]{2,1,0:T(8,128)(2,1)} %constant_dynamic-slice_fusion.10), channel_id=1, source_target_pairs={{0,4},{4,0},{8,12},{12,8},{16,20},{20,16},{24,28},{28,24},{1,5},{5... | collective-permute-start | bytes 1572872 | tf_op jit(solution)/shard_map/ppermute | solution.py:15
  18.0 48.9 %copy-start.26 = (f32[16,128]{1,0:T(8,128)}, f32[16,128]{1,0:T(8,128)S(1)}, u32[]{:S(2)}) copy-start(f32[16,128]{1,0:T(8,128)S(1)} %convert_subtract_fusion) | copy-start | bytes 24580
  66.9 2.0 copy-start.10
  259.6 158.5 %copy-start.14 = (f32[16,128,128]{2,1,0:T(8,128)}, f32[16,128,128]{2,1,0:T(8,128)S(1)}, u32[]{:S(2)}) copy-start(f32[16,128,128]{2,1,0:T(8,128)S(1)} %get-tuple-element.109) | copy-start | bytes 3145732
  259.6 160.3 %copy-start.2 = (bf16[16,2,128,128]{3,2,1,0:T(8,128)(2,1)S(1)}, bf16[16,2,128,128]{3,2,1,0:T(8,128)(2,1)}, u32[]{:S(2)}) copy-start(bf16[16,2,128,128]{3,2,1,0:T(8,128)(2,1)} %copy-done.1) | copy-start | bytes 3145732
  418.0 9.0 collective-permute-start
  420.0 1.0 copy-start.6
  420.0 1.6 copy-start.13
  420.0 1.9 copy-start.15
  421.9 408.3 %copy-start = (f32[16,2,128,128]{3,2,1,0:T(8,128)}, f32[16,2,128,128]{3,2,1,0:T(8,128)S(1)}, u32[]{:S(2)}) copy-start(f32[16,2,128,128]{3,2,1,0:T(8,128)S(1)} %fusion.34) | copy-start | bytes 6291460
  427.0 2.9 copy-start.24
  427.0 1.9 copy-start.16
  429.0 1.0 copy-start.4
  440.9 1.3 copy-start.8
  538.3 2.7 copy-start.9
  538.3 2.7 copy-start.17
  538.3 2.7 copy-start.23
  830.2 5.4 copy-start.7
  830.2 5.4 copy-start.11
  835.6 3.4 copy-start.30
  835.6 3.5 copy-start.3
  1083.8 3.2 copy-start.19
  1085.9 2.1 copy-start.5
  1086.0 2.1 copy-start.25
  1088.1 3.1 copy-start.22
  1094.0 6.7 collective-permute-start.2
  1097.8 2.9 copy-start.18
Sparse Core Ops, SparseCore 0:
  11.6 55.2 all-reduce.4
  69.3 35.4 all-gather.4
  106.7 52.8 all-gather.2
  839.1 61.6 all-reduce.6
where the time goes:
time: 1130 us; the launch traced here: 1120 us
  other arithmetic  887 us (78%)
  matrix products  103 us (9%)
  local copies, waits for them, and re-layouts  61.7 us (5%)
  waiting for transfers between devices  46.7 us (4%)
  between operations  14.8 us (1%)
    another operation x11, other arithmetic, lower_inverse(): factor_low = jnp.linalg.cholesky(matrix)  461 us
    another operation x7, other arithmetic, lower_inverse(): jax.scipy.linalg.solve_triangular(factor_low, identity, lower=True)  323 us
    another operation x2, other arithmetic, per_device(): jax.scipy.linalg.solve_triangular(far_low, far_identity, lower=True)  81.3 us
    dot_general x24, matrix products, kernel_apply(): jnp.einsum('vnwp,wpk->vnk', matern(near_coords, far_coords), far_columns,...  53.1 us
    psum x1, waiting for transfers between devices, per_device(): lax.psum(local_gram, 'gen') + jax.vmap(jnp.diag)(1.0 - column_keep)  44.4 us
  transfers between devices with their start and end apart: 9, of which 2 were waited for; matrix products, arithmetic and copies ran while one was open for 86% of the time, Pallas kernels for 0%

commit v1 on v0

--- a/solution.py
+++ b/solution.py
@@ -69,7 +69,9 @@
     far_coords = swapped(coords, "leaf", 0)
     own_far_coords = select_half(far_coords, keep_start)
     local_gram = jnp.einsum("lvnk,lvnj->lkj", masked, masked, preferred_element_type=jnp.float32)
-    gram_sum = lax.psum(local_gram, "gen") + jax.vmap(jnp.diag)(1.0 - column_keep)
+    gram_sum = jnp.sum(lax.all_gather(local_gram, "gen"), axis=0) + jax.vmap(jnp.diag)(
+        1.0 - column_keep
+    )
     lows, inverses = lower_inverse(gram_sum)
     bases = jnp.einsum(
         "lvnk,ljk->lvnj", masked, inverses, precision=HIGHEST, preferred_element_type=jnp.float32

time: 1130 us -> 1120 us (level)
  waiting for transfers between devices: 46.7 us -> 68.9 us
  local copies, waits for them, and re-layouts: 61.7 us -> 47.8 us
    psum x1 -> x0, waiting for transfers between devices: 44.4 us -> none  [per_device(): lax.psum(local_gram, 'gen') + jax.vmap(jnp.diag)(1.0 - column_keep)]
    all_gather x0 -> x1, waiting for transfers between devices: none -> 38.8 us  [per_device(): lax.all_gather(local_gram, 'gen')]
    all_gather x1, waiting for transfers between devices: 0.01 us -> 27.7 us  [per_device(): piece_far = lax.all_gather(far_shards, 'gen', axis=2, tiled=True)]
  transfers between devices with their start and end apart: 9 -> 9, of which waited for: 2 -> 3; matrix products, arithmetic and copies ran while one was open for 86% -> 91% of each run, Pallas kernels for 0% -> 0%
where the time goes in v1:
time: 1120 us; the launch traced here: 1110 us
  other arithmetic  886 us (79%)
  matrix products  93.4 us (8%)
  waiting for transfers between devices  68.9 us (6%)
  local copies, waits for them, and re-layouts  47.8 us (4%)
  between operations  14.8 us (1%)
    another operation x11, other arithmetic, lower_inverse(): factor_low = jnp.linalg.cholesky(matrix)  460 us
    another operation x7, other arithmetic, lower_inverse(): jax.scipy.linalg.solve_triangular(factor_low, identity, lower=True)  321 us
    another operation x2, other arithmetic, per_device(): jax.scipy.linalg.solve_triangular(far_low, far_identity, lower=True)  82.4 us
    dot_general x24, matrix products, kernel_apply(): jnp.einsum('vnwp,wpk->vnk', matern(near_coords, far_coords), far_columns,...  48 us
    all_gather x1, waiting for transfers between devices, per_device(): lax.all_gather(local_gram, 'gen')  38.8 us
    all_gather x1, waiting for transfers between devices, per_device(): piece_far = lax.all_gather(far_shards, 'gen', axis=2, tiled=True)  27.7 us
  transfers between devices with their start and end apart: 9, of which 3 were waited for; matrix products, arithmetic and copies ran while one was open for 91% of the time, Pallas kernels for 0%

profile of v1, /device:TPU:0, one launch (start us, length us, event | category | flops | bytes accessed | tf_op | source)
XLA Modules:
  0.0 1113.6 jit_solution(1196303056148546845)
XLA Ops:
  22.6 27.7 %all-gather.7.cloned.1.call-done = bf16[8,2,512,128]{3,2,1,0:T(8,128)(2,1)} async-done(((bf16[8,2,128,128]{3,2,1,0:T(8,128)(2,1)}), bf16[8,2,512,128]{3,2,1,0:T(8,128)(2,1)}) %all-gather.7.cloned.1.call-update) | async-done | bytes 2097168 | tf_op jit(solution)/shard_map/all_gather | solution.py:85
  50.3 16.3 %while.22 = (s32[]{:T(128)}, f32[8,2,128,128]{3,2,1,0:T(8,128)S(1)}, f32[8,2,128]{2,1,0:T(2,128)S(1)}, f32[8,2,512]{2,1,0:T(2,128)S(1)}, bf16[8,2,512,128]{3,2,1,0:T(8,128)(2,1)}, /*index=5*/s32[]{:T(128)}, s32[]{:T(128)}, s32[]{}) while((s32[]{:T(128)}, f32[8,2,128,128]{3,2,1,0:T(8,128)S(1)}, f32[8,2,128]{2,1,0:T(2,128)S(1)}, ...), condition=%wide.region_11.12_spmd, body=%wide.region_10.11_spmd.sunk | while | flops 404160512 | bytes 4081781 | solution.py:87
  66.6 38.8 %all-gather.9.cloned.1.call-done = f32[64,128,128]{2,1,0:T(8,128)} async-done(((f32[16,128,128]{2,1,0:T(8,128)}), f32[64,128,128]{2,1,0:T(8,128)}) %all-gather.9.cloned.1.call-update) | async-done | bytes 4194320 | tf_op jit(solution)/shard_map/all_gather | solution.py:72
  105.4 2.6 reduce_sum.11
  109.5 187.5 %custom-call.29 = f32[16,128,128]{2,1,0:T(8,128)S(1)} custom-call(f32[16,128,128]{2,1,0:T(8,128)S(1)} %fusion.39), custom_call_target="Cholesky" | custom-call | tf_op jit(solution)/shard_map/jit(cholesky)/cholesky | solution.py:43
  297.3 2.0 select_bitcast_fusion
  299.3 157.3 %custom-call.30 = f32[16,1,128,128]{2,3,1,0:T(8,128)S(1)} custom-call(f32[16,1,128,128]{3,2,1,0:T(8,128)S(1)} %get-tuple-element.112), custom_call_target="InvertDiagBlocksLowerTriangular" | custom-call | tf_op jit(solution)/shard_map/jit(_solve_triangular)/vmap()/triangular_solve | solution.py:45
  460.5 3.5 fusion.33
  464.0 65.3 %while.21 = (s32[]{:T(128)}, f32[16,2,128,128]{3,2,1,0:T(8,128)}, f32[16,2,128]{2,1,0:T(2,128)}, f32[16,2,512]{2,1,0:T(2,128)}, bf16[16,2,512,128]{3,2,1,0:T(8,128)(2,1)}, /*index=5*/s32[]{:T(128)}, s32[]{:T(128)}, s32[]{}) while((s32[]{:T(128)}, f32[16,2,128,128]{3,2,1,0:T(8,128)}, f32[16,2,128]{2,1,0:T(2,128)}, f32[16,2,512]{2,1,0:T(2,128)}, ...), condition=%wide.region_4.5_spmd, body=%wide.region_3.4_spmd.sunk | while | flops 404160512 | bytes 4081781 | solution.py:86
  465.9 2.2 fusion.99
  469.9 2.2 fusion.99
  474.0 2.2 fusion.99
  478.0 2.2 fusion.99
  482.1 2.2 fusion.99
  486.1 2.2 fusion.99
  490.2 2.2 fusion.99
  494.3 2.2 fusion.99
  498.3 2.2 fusion.99
  502.4 2.2 fusion.99
  506.4 2.2 fusion.99
  510.5 2.2 fusion.99
  514.6 2.2 fusion.99
  518.6 2.2 fusion.99
  522.7 2.2 fusion.99
  526.7 2.2 fusion.99
  529.3 5.3 convolution_bitcast_fusion.3
  535.5 2.7 convolution_bitcast_fusion.5
  538.2 3.3 convolution_add_fusion
  545.1 3.6 fusion.32
  548.7 2.0 copy.50
  550.7 2.1 fusion.31
  554.2 94.5 %custom-call.31 = f32[8,128,128]{2,1,0:T(8,128)} custom-call(f32[8,128,128]{2,1,0:T(8,128)S(1)} %cholesky.145), custom_call_target="Cholesky" | custom-call | tf_op jit(solution)/shard_map/jit(cholesky)/cholesky | solution.py:43
  650.0 2.1 select_bitcast_fusion.1
  652.1 80.0 %custom-call.32 = f32[8,1,128,128]{2,3,1,0:T(8,128)} custom-call(f32[8,1,128,128]{3,2,1,0:T(8,128)} %get-tuple-element.144), custom_call_target="InvertDiagBlocksLowerTriangular" | custom-call | tf_op jit(solution)/shard_map/jit(cholesky)/cholesky | solution.py:43
  734.0 3.1 convolution_subtract_fusion.1
  737.1 95.4 %custom-call.33 = f32[8,128,128]{2,1,0:T(8,128)} custom-call(f32[8,128,128]{2,1,0:T(8,128)} %convolution_subtract_fusion.1), custom_call_target="Cholesky" | custom-call | tf_op jit(solution)/shard_map/jit(cholesky)/cholesky | solution.py:43
  835.2 1.9 select_select_fusion
  837.2 5.8 while.23
  837.8 2.3 bitcast_dynamic-update-slice_fusion.2
  840.7 2.3 bitcast_dynamic-update-slice_fusion.2
  843.0 158.6 %custom-call.34 = f32[8,2,128,128]{2,3,1,0:T(8,128)} custom-call(f32[8,2,128,128]{3,2,1,0:T(8,128)} %bitcast.192), custom_call_target="InvertDiagBlocksLowerTriangular" | custom-call | tf_op jit(solution)/shard_map/jit(_solve_triangular)/vmap()/triangular_solve | solution.py:45
  1001.6 80.3 %custom-call.35 = f32[8,1,128,128]{2,3,1,0:T(8,128)} custom-call(f32[8,1,128,128]{3,2,1,0:T(8,128)} %get-tuple-element.143), custom_call_target="InvertDiagBlocksLowerTriangular" | custom-call | tf_op jit(solution)/shard_map/jit(_solve_triangular)/vmap()/triangular_solve | solution.py:101
  1081.9 2.2 fusion.45
  1086.2 2.2 fusion.18
  1090.3 1.9 constant_dynamic-slice_fusion.9
  1092.7 2.3 fusion.67
  1100.1 2.2 fusion.22
  1102.2 3.5 fusion.68
  (255 shorter events, 88.9 us)
Async XLA Ops:
  7.2 43.1 %all-gather.7.cloned.1.call-start = ((), (), s32[]{:S(2)}) async-start(), calls=%async_computation.1 | async-start | bytes 2621440 | tf_op jit(solution)/shard_map/all_gather | solution.py:85
  9.2 4.5 copy-start.1
  9.3 2.1 collective-permute-start.4
  11.4 0.8 copy-start.19
  12.2 2.4 copy-start.23
  12.2 2.8 copy-start.16
  12.2 93.2 %all-gather.9.cloned.1.call-start = ((), (), s32[]{:S(2)}) async-start(), calls=%async_computation.2 | async-start | bytes 5242880 | tf_op jit(solution)/shard_map/all_gather | solution.py:72
  13.7 4.2 copy-start.24
  13.8 5.5 copy-start.25
  13.8 450.2 %all-gather.5.cloned.1.call-start = ((), (), s32[]{:S(2)}) async-start(), calls=%async_computation | async-start | bytes 5242880 | tf_op jit(solution)/shard_map/all_gather | solution.py:84
  14.5 1075.8 %all-reduce.4.cloned.1.call-start = ((), (), s32[]{:S(2)}) async-start(), calls=%async_computation.3 | async-start | bytes 3145728 | tf_op jit(solution)/shard_map/psum | solution.py:96
  14.6 8.0 collective-permute-start.3
  15.3 1.0 copy-start.10
  17.2 525.1 %collective-permute-start.1 = (bf16[8,128,256]{2,1,0:T(8,128)(2,1)}, bf16[8,128,256]{2,1,0:T(8,128)(2,1)}, u32[]{:S(2)}, u32[]{:S(2)}) collective-permute-start(bf16[8,128,256]{2,1,0:T(8,128)(2,1)} %constant_dynamic-slice_fusion.10), channel_id=1, source_target_pairs={{0,4},{4,0},{8,12},{12,8},{16,20},{20,16},{24,28},{28,24},{1,5},{5... | collective-permute-start | bytes 1572872 | tf_op jit(solution)/shard_map/ppermute | solution.py:15
  66.6 38.8 %copy-start.17 = (f32[8,2,128,128]{3,2,1,0:T(8,128)}, f32[8,2,128,128]{3,2,1,0:T(8,128)S(1)}, u32[]{:S(2)}) copy-start(f32[8,2,128,128]{3,2,1,0:T(8,128)S(1)} %get-tuple-element.59) | copy-start | bytes 3145732
  297.3 162.2 %copy-start.2 = (bf16[16,2,128,128]{3,2,1,0:T(8,128)(2,1)S(1)}, bf16[16,2,128,128]{3,2,1,0:T(8,128)(2,1)}, u32[]{:S(2)}) copy-start(bf16[16,2,128,128]{3,2,1,0:T(8,128)(2,1)} %copy-done.1) | copy-start | bytes 3145732
  458.4 1.0 copy-start.5
  460.4 75.1 %copy-start = (f32[16,2,128,128]{3,2,1,0:T(8,128)}, f32[16,2,128,128]{3,2,1,0:T(8,128)S(1)}, u32[]{:S(2)}) copy-start(f32[16,2,128,128]{3,2,1,0:T(8,128)S(1)} %fusion.34) | copy-start | bytes 6291460
  529.3 5.4 copy-start.12
  529.3 6.2 copy-start.18
  534.7 3.5 copy-start.6
  535.5 6.7 collective-permute-start
  538.2 3.3 copy-start.11
  538.2 3.3 copy-start.13
  542.2 2.9 copy-start.21
  544.1 1.0 copy-start.3
  552.8 1.4 copy-start.8
  648.7 1.3 copy-start.9
  833.8 1.4 copy-start.7
  835.1 1.9 copy-start.26
  1081.9 3.2 copy-start.15
  1084.1 2.1 copy-start.4
  1084.1 2.1 copy-start.22
  1086.2 3.1 copy-start.20
  1092.2 6.7 collective-permute-start.2
  1096.0 2.9 copy-start.14
Sparse Core Ops, SparseCore 0:
  12.3 37.9 all-gather.6
  52.7 52.6 all-gather.8
  107.3 52.8 all-gather.4
  541.7 61.5 all-reduce.3
